TPU v7x, 128 devices: a whole 4x4x4 slice. The times are simulated.
128 devices in a mesh: loader: 4 (over z_hi, core), centers: 32 (over y, z_lo, x).
Axes of the slice: x: 4, y: 4, z: 4 (z_hi: 2, z_lo: 2; z = z_hi * 2 + z_lo), core: 2. Of those that a mesh axis runs over, the one named last changes fastest.
Arguments:
- pool: bfloat16 [32768, 256], P('loader'), may hold values from -6 to 6
- batch_index: int32 [2048], replicated, may hold values from 0 to 32767
- targets: float32 [16, 2048], replicated, may hold values from -6 to 6
- centers: bfloat16 [1048576, 256], P(('loader', 'centers')), may hold values from -6 to 6
- weights: float32 [16, 1048576], P(None, ('loader', 'centers')), may hold values from -1.8 to 1.8
- nys_index: int32 [8192], P(('loader', 'centers')), may hold values from 0 to 8191, as said below
- eigvecs: float32 [8192, 128], P(('loader', 'centers')), may hold values from -0.0625 to 0.0625
- damping: float32 [128], replicated, may hold values from 1 to 30
Outputs:
- new_weights: float32 [16, 1048576], P(None, ('loader', 'centers'))
- predictions: float32 [16, 2048], replicated
Inputs may be any that keep to these rules, and one draw needn't show every extreme that they name: `nys_index`: each device's block of 64 entries names distinct local rows of that device's own 8192 centers; entry k lies in [k * 128, (k + 1) * 128); the first is 0 and the last 8191.
All inputs are finite; a program needn't handle non-finite values.
Results may differ from a plain program's by a relative error of at most 0.0049.
Values may be sent and summed in bfloat16 or wider, within the bound.
No kernel may reach another device: no remote copies, remote signals or barrier semaphores. Data moves between devices by JAX's collectives and lax.ppermute only.
A program may use at most 256 MiB of HBM per device.

v0:
```python
import math
import jax
import jax.numpy as jnp
from jax import lax
from jax.sharding import PartitionSpec as P

D = 256


def pick_rows(pool, wanted):
    held = pool.shape[0]
    local = wanted - lax.axis_index("loader") * held
    owned = (local >= 0) & (local < held)
    rows = pool[jnp.clip(local, 0, held - 1)]
    return jnp.where(owned[:, None], rows, jnp.zeros_like(rows))


def body(pool, batch_index, targets, centers, weights, nys_index, eigvecs, damping):
    total_rows = batch_index.shape[0]
    share = total_rows // lax.axis_size("centers")
    mine = lax.dynamic_slice_in_dim(batch_index, lax.axis_index("centers") * share, share)
    summed = lax.psum(pick_rows(pool, mine), "loader").astype(jnp.float32).astype(jnp.bfloat16)
    batch = lax.all_gather(summed, "centers", axis=0, tiled=True)
    cen_sq = jnp.sum(centers.astype(jnp.float32) * centers.astype(jnp.float32), axis=1)
    width = min(512, total_rows)

    def tile(rows):
        row_sq = jnp.sum(rows.astype(jnp.float32) * rows.astype(jnp.float32), axis=1)
        cross = jnp.dot(rows, centers.T, preferred_element_type=jnp.float32)
        dist_sq = row_sq[:, None] + cen_sq[None, :] - 2.0 * cross
        return jnp.exp(-4.0 * jnp.sqrt(dist_sq) / math.sqrt(D)).astype(jnp.bfloat16)

    kern = lax.map(tile, batch.reshape(total_rows // width, width, batch.shape[1]))
    kern = kern.reshape(total_rows, centers.shape[0])
    w_half = weights.astype(jnp.bfloat16)
    partial_value = lax.dot_general(
        w_half, kern, (((1,), (1,)), ((), ())), preferred_element_type=jnp.float32
    )
    predictions = lax.psum(partial_value, ("loader", "centers"))
    resid = (predictions - targets).astype(jnp.bfloat16)
    grad = jnp.dot(resid, kern, preferred_element_type=jnp.float32)
    grad_nys = grad[:, nys_index]
    local_coeff = jnp.dot(
        grad_nys, eigvecs, precision=lax.Precision.HIGHEST, preferred_element_type=jnp.float32
    )
    coeff = lax.psum(local_coeff, ("loader", "centers"))
    delta = jnp.dot(
        coeff * damping[None, :],
        eigvecs.T,
        precision=lax.Precision.HIGHEST,
        preferred_element_type=jnp.float32,
    )
    fresh = weights - 2.0 * grad
    fresh = fresh.at[:, nys_index].add(2.0 * delta)
    return (fresh, predictions)


def solution(mesh):
    return jax.shard_map(
        body,
        mesh=mesh,
        in_specs=(
            P("loader", None),
            P(),
            P(),
            P(("loader", "centers"), None),
            P(None, ("loader", "centers")),
            P(("loader", "centers")),
            P(("loader", "centers"), None),
            P(),
        ),
        out_specs=(P(None, ("loader", "centers")), P()),
        check_vma=False,
    )
```

profile of v0, /device:TPU:1, one launch (start us, length us, event | category | flops | bytes accessed | tf_op | source)
XLA Modules:
  0.0 498.1 jit_solution(4399989665971109694)
XLA Ops:
  7.2 0.0 copy-start
  7.2 0.0 all-gather.2.cloned.1.call-start
  7.2 0.8 compare_select_fusion.1
  8.0 0.8 compare_and_fusion
  8.8 3.4 gather_fusion
  12.2 0.1 broadcast_select_fusion
  12.2 15.6 %psum.21 = bf16[64,256]{1,0:T(8,128)(2,1)} all-reduce(bf16[64,256]{1,0:T(8,128)(2,1)S(1)} %broadcast_select_fusion), channel_id=1, replica_groups=mesh['loader'=4,'centers'=32] {'loader'}, use_global_device_ids=true, to_apply=%region_0.1 | all-reduce | flops 16384 | bytes 65536 | tf_op jit(solution)/shard_map/psum | solution.py:22
  27.9 0.0 all-gather.2.cloned.1.call-update
  27.9 0.0 all-reduce.2.cloned.1.call-start
  28.0 0.7 compare_select_fusion
  28.6 3.3 multiply_reduce_fusion.1
  32.0 127.5 %all-gather.2.cloned.1.call-done = bf16[2048,256]{1,0:T(8,128)(2,1)} async-done(((bf16[64,256]{1,0:T(8,128)(2,1)}), bf16[2048,256]{1,0:T(8,128)(2,1)}) %all-gather.2.cloned.1.call-update) | async-done | bytes 1048592 | tf_op jit(solution)/shard_map/all_gather | solution.py:23
  159.5 0.0 copy-start.1
  159.5 58.4 %while.12 = (s32[]{:T(128)}, bf16[4,512,8192]{2,1,0:T(8,128)(2,1)}, bf16[4,512,256]{2,1,0:T(8,128)(2,1)}, f32[8192]{0:T(1024)S(1)}, bf16[8192,256]{1,0:T(8,128)(2,1)}, /*index=5*/s32[]{:T(128)}) while((s32[]{:T(128)}, bf16[4,512,8192]{2,1,0:T(8,128)(2,1)}, bf16[4,512,256]{2,1,0:T(8,128)(2,1)}, f32[8192]{0:T(1024)S(1)}, ...), condition=%wide.region_4.5_spmd, body=%wide.region_2.4_spmd.sunk | while | flops 2168847872 | bytes 13145161 | solution.py:33
  159.5 1.2 multiply_reduce_fusion.3
  160.6 13.5 %fusion.22 = bf16[4,512,8192]{2,1,0:T(8,128)(2,1)} fusion(bf16[4,512,8192]{2,1,0:T(8,128)(2,1)} %get-tuple-element.120, s32[]{:T(128)} %get-tuple-element.119, bf16[8192,256]{1,0:T(8,128)(2,1)} %get-tuple-element.129, f32[8192]{0:T(1024)S(1)} %get-tuple-element.128, f32[512]{0:T(512)S(1)} %multiply_reduce_fusion.3, ...), kind=kOutput, calls=%fused_computation.5.clone.1 | convolution fusion | flops 2168455168 | bytes 12880896 | tf_op jit(solution)/shard_map/while/body/eval_jaxpr/dot_general | solution.py:29
  174.1 1.1 multiply_reduce_fusion.3
  175.2 13.5 %fusion.22 = bf16[4,512,8192]{2,1,0:T(8,128)(2,1)} fusion(bf16[4,512,8192]{2,1,0:T(8,128)(2,1)} %get-tuple-element.120, s32[]{:T(128)} %get-tuple-element.119, bf16[8192,256]{1,0:T(8,128)(2,1)} %get-tuple-element.129, f32[8192]{0:T(1024)S(1)} %get-tuple-element.128, f32[512]{0:T(512)S(1)} %multiply_reduce_fusion.3, ...), kind=kOutput, calls=%fused_computation.5.clone.1 | convolution fusion | flops 2168455168 | bytes 12880896 | tf_op jit(solution)/shard_map/while/body/eval_jaxpr/dot_general | solution.py:29
  188.7 1.1 multiply_reduce_fusion.3
  189.8 13.5 %fusion.22 = bf16[4,512,8192]{2,1,0:T(8,128)(2,1)} fusion(bf16[4,512,8192]{2,1,0:T(8,128)(2,1)} %get-tuple-element.120, s32[]{:T(128)} %get-tuple-element.119, bf16[8192,256]{1,0:T(8,128)(2,1)} %get-tuple-element.129, f32[8192]{0:T(1024)S(1)} %get-tuple-element.128, f32[512]{0:T(512)S(1)} %multiply_reduce_fusion.3, ...), kind=kOutput, calls=%fused_computation.5.clone.1 | convolution fusion | flops 2168455168 | bytes 12880896 | tf_op jit(solution)/shard_map/while/body/eval_jaxpr/dot_general | solution.py:29
  203.3 1.1 multiply_reduce_fusion.3
  204.4 13.5 %fusion.22 = bf16[4,512,8192]{2,1,0:T(8,128)(2,1)} fusion(bf16[4,512,8192]{2,1,0:T(8,128)(2,1)} %get-tuple-element.120, s32[]{:T(128)} %get-tuple-element.119, bf16[8192,256]{1,0:T(8,128)(2,1)} %get-tuple-element.129, f32[8192]{0:T(1024)S(1)} %get-tuple-element.128, f32[512]{0:T(512)S(1)} %multiply_reduce_fusion.3, ...), kind=kOutput, calls=%fused_computation.5.clone.1 | convolution fusion | flops 2168455168 | bytes 12880896 | tf_op jit(solution)/shard_map/while/body/eval_jaxpr/dot_general | solution.py:29
  217.9 0.0 copy-done.1
  217.9 0.0 copy-start.3
  217.9 15.7 %convolution_bitcast_fusion = f32[16,2048]{1,0:T(8,128)} fusion(bf16[2048,8192]{1,0:T(8,128)(2,1)} %bitcast.28, f32[16,8192]{1,0:T(8,128)S(1)} %copy-done.1), kind=kOutput, calls=%fused_computation.11 | convolution fusion | flops 537001984 | bytes 34209792 | tf_op jit(solution)/shard_map/dot_general | solution.py:36
  233.6 0.0 all-reduce.2.cloned.1.call-update
  233.6 0.0 copy-start.4
  233.6 161.8 %all-reduce.2.cloned.1.call-done = f32[16,2048]{1,0:T(8,128)} async-done(((f32[16,2048]{1,0:T(8,128)}), f32[16,2048]{1,0:T(8,128)}) %all-reduce.2.cloned.1.call-update) | async-done | bytes 131088 | tf_op jit(solution)/shard_map/psum | solution.py:39
  395.4 0.0 copy-done.3
  395.4 0.0 copy-start.2
  395.4 14.8 %multiply_subtract_fusion = (f32[16,8192]{1,0:T(8,128)S(1)}, f32[16,8192]{1,0:T(8,128)S(1)}) fusion(f32[16,8192]{1,0:T(8,128)S(1)} %copy-done.1, bf16[2048,8192]{1,0:T(8,128)(2,1)} %bitcast.29, f32[16,2048]{1,0:T(8,128)} %all-reduce.2.cloned.1.call-done, f32[16,2048]{1,0:T(8,128)S(1)} %copy-done.3), kind=kOutput, calls=%fused_computation.14 | convolution fusion | flops 537198592 | bytes 35389440 | tf_op jit(solution)/shard_map/dot_general | solution.py:41
  410.3 2.6 copy.10
  412.9 2.8 gather_fusion.1
  415.7 0.0 copy-done
  415.7 0.2 fusion.10
  415.9 63.4 %psum.23 = f32[16,128]{1,0:T(8,128)S(1)} all-reduce(f32[16,128]{1,0:T(8,128)S(1)} %fusion.10), channel_id=1, replica_groups=mesh['loader'=4,'centers'=32] {'loader','centers'}, use_global_device_ids=true, to_apply=%region_6.7 | all-reduce | flops 2048 | bytes 16384 | tf_op jit(solution)/shard_map/psum | solution.py:46
  479.3 0.0 copy-done.4
  479.3 0.1 fusion.5
  479.4 0.1 copy.12
  479.5 2.6 copy.11
  482.1 4.9 scatter_fusion
  487.1 3.5 copy.13
  490.6 0.0 copy-done.2
  490.6 0.7 copy.25
  (3 shorter events, 0.0 us)
Async XLA Ops:
  7.2 408.5 %copy-start = (f32[64,128]{1,0:T(8,128)S(1)}, f32[64,128]{1,0:T(8,128)}, u32[]{:S(2)}) copy-start(f32[64,128]{1,0:T(8,128)} %param.16) | copy-start | bytes 98308
  7.2 152.3 %all-gather.2.cloned.1.call-start = ((), (), s32[]{:S(2)}) async-start(), calls=%async_computation | async-start | bytes 1081344 | tf_op jit(solution)/shard_map/all_gather | solution.py:23
  27.9 367.5 %all-reduce.2.cloned.1.call-start = ((), (), s32[]{:S(2)}) async-start(), calls=%async_computation.1 | async-start | bytes 262144 | tf_op jit(solution)/shard_map/psum | solution.py:39
  159.5 58.4 %copy-start.1 = (f32[16,8192]{1,0:T(8,128)S(1)}, f32[16,8192]{1,0:T(8,128)}, u32[]{:S(2)}) copy-start(f32[16,8192]{1,0:T(8,128)} %param.14) | copy-start | bytes 1572868
  217.9 177.5 %copy-start.3 = (f32[16,2048]{1,0:T(8,128)S(1)}, f32[16,2048]{1,0:T(8,128)}, u32[]{:S(2)}) copy-start(f32[16,2048]{1,0:T(8,128)} %param.12) | copy-start | bytes 393220
  233.6 245.7 %copy-start.4 = (f32[128]{0:T(128)S(1)}, f32[128]{0:T(128)}, u32[]{:S(2)}) copy-start(f32[128]{0:T(128)} %param.17) | copy-start | bytes 1540
  395.4 95.2 %copy-start.2 = (f32[16,2048]{1,0:T(8,128)S(1)}, f32[16,2048]{1,0:T(8,128)}, u32[]{:S(2)}) copy-start(f32[16,2048]{1,0:T(8,128)} %all-reduce.2.cloned.1.call-done) | copy-start | bytes 393220
Sparse Core Ops, SparseCore 0:
  28.0 131.4 all-gather.1
  233.7 161.6 all-reduce.1
where the time goes:
time: 499 us; the launch traced here: 498 us
  waiting for transfers between devices  289 us (58%)
  matrix products  84.8 us (17%)
  blocking collectives  79.1 us (16%)
  local copies, waits for them, and re-layouts  15.7 us (3%)
  other arithmetic  15 us (3%)
  between operations  14.1 us (3%)
    psum x1, waiting for transfers between devices, body(): predictions = lax.psum(partial_value, ('loader', 'centers'))  162 us
    all_gather x1, waiting for transfers between devices, body(): batch = lax.all_gather(summed, 'centers', axis=0, tiled=True)  128 us
    psum x1, blocking collectives, body(): coeff = lax.psum(local_coeff, ('loader', 'centers'))  63.4 us
    dot_general x4, matrix products, tile(): cross = jnp.dot(rows, centers.T, preferred_element_type=jnp.float32)  54 us
    dot_general x1, matrix products, body(): lax.dot_general(w_half, kern, (((1,), (1,)), ((), ())), preferred_element...  15.7 us
    psum x1, blocking collectives, body(): lax.psum(pick_rows(pool, mine), 'loader').astype(jnp.float32)  15.6 us
    dot_general x1, matrix products, body(): grad = jnp.dot(resid, kern, preferred_element_type=jnp.float32)  14.8 us
  transfers between devices with their start and end apart: 2, of which 2 were waited for; matrix products, arithmetic and copies ran while one was open for 1% of the time, Pallas kernels for 0%

commit v1 on v0

--- a/solution.py
+++ b/solution.py
@@ -20,7 +20,9 @@
     share = total_rows // lax.axis_size("centers")
     mine = lax.dynamic_slice_in_dim(batch_index, lax.axis_index("centers") * share, share)
     summed = lax.psum(pick_rows(pool, mine), "loader").astype(jnp.float32).astype(jnp.bfloat16)
-    batch = lax.all_gather(summed, "centers", axis=0, tiled=True)
+    batch = jnp.concatenate(
+        lax.all_to_all(jnp.stack([summed] * lax.axis_size("centers")), "centers", 0, 0), axis=0
+    )
     cen_sq = jnp.sum(centers.astype(jnp.float32) * centers.astype(jnp.float32), axis=1)
     width = min(512, total_rows)
 

time: 499 us -> 362 us (0.73)
  waiting for transfers between devices: 289 us -> 153 us
  starting transfers between devices: 0.08 us -> 7.69 us
    all_gather x1 -> x0, waiting for transfers between devices: 128 us -> none  [body(): batch = lax.all_gather(summed, 'centers', axis=0, tiled=True)]
    psum x1, waiting for transfers between devices: 162 us -> 143 us  [body(): predictions = lax.psum(partial_value, ('loader', 'centers'))]
    all_to_all x0 -> x1, waiting for transfers between devices: none -> 9.48 us  [body(): lax.all_to_all(jnp.stack([summed] * lax.axis_size('centers')), 'centers',...]
    all_to_all x0 -> x1, starting transfers between devices: none -> 7.65 us  [body(): lax.all_to_all(jnp.stack([summed] * lax.axis_size('centers')), 'centers',...]
where the time goes in v1:
time: 362 us
  waiting for transfers between devices  153 us (42%)
  matrix products  81.1 us (22%)
  blocking collectives  78.5 us (22%)
  local copies, waits for them, and re-layouts  16.8 us (5%)
  between operations  14.1 us (4%)
  other arithmetic  11.2 us (3%)
  starting transfers between devices  7.69 us (2%)
    psum x1, waiting for transfers between devices, body(): predictions = lax.psum(partial_value, ('loader', 'centers'))  143 us
    psum x1, blocking collectives, body(): coeff = lax.psum(local_coeff, ('loader', 'centers'))  63.4 us
    dot_general x4, matrix products, tile(): cross = jnp.dot(rows, centers.T, preferred_element_type=jnp.float32)  50.2 us
    dot_general x1, matrix products, body(): lax.dot_general(w_half, kern, (((1,), (1,)), ((), ())), preferred_element...  15.7 us
    psum x1, blocking collectives, body(): lax.psum(pick_rows(pool, mine), 'loader').astype(jnp.float32)  15 us
    dot_general x1, matrix products, body(): grad = jnp.dot(resid, kern, preferred_element_type=jnp.float32)  14.8 us
    all_to_all x1, waiting for transfers between devices, body(): lax.all_to_all(jnp.stack([summed] * lax.axis_size('centers')), 'centers',...  9.48 us
    all_to_all x1, starting transfers between devices, body(): lax.all_to_all(jnp.stack([summed] * lax.axis_size('centers')), 'centers',...  7.65 us
  transfers between devices with their start and end apart: 2, of which 2 were waited for; matrix products, arithmetic and copies ran while one was open for 1% of the time, Pallas kernels for 0%

profile of v1, /device:TPU:1, one launch (start us, length us, event | category | flops | bytes accessed | tf_op | source)
XLA Modules:
  0.0 361.8 jit_solution(13290372165352687629)
XLA Ops:
  7.2 0.0 copy-start
  7.2 0.8 compare_select_fusion.1
  8.0 0.8 compare_and_fusion
  8.7 3.4 gather_fusion
  12.1 0.1 broadcast_select_fusion
  12.2 15.0 %psum.21 = bf16[64,256]{1,0:T(8,128)(2,1)S(1)} all-reduce(bf16[64,256]{1,0:T(8,128)(2,1)S(1)} %broadcast_select_fusion), channel_id=1, replica_groups=mesh['loader'=4,'centers'=32] {'loader'}, use_global_device_ids=true, to_apply=%region_0.1 | all-reduce | flops 16384 | bytes 65536 | tf_op jit(solution)/shard_map/psum | solution.py:22
  27.2 1.1 stack.2
  28.3 7.6 %all-to-all-start = ((bf16[32,64,256]{2,1,0:T(8,128)(2,1)}), bf16[32,64,256]{2,1,0:T(8,128)(2,1)S(1)}, u32[]{:S(2)}, u32[]{:S(2)}) async-start(bf16[32,64,256]{2,1,0:T(8,128)(2,1)} %stack.2), calls=%async_computation | async-start | bytes 2097152 | tf_op jit(solution)/shard_map/all_to_all | solution.py:24
  36.0 0.0 all-reduce.2.cloned.1.call-start
  36.1 0.7 compare_select_fusion
  36.7 3.3 multiply_reduce_fusion.1
  40.1 9.5 %all-to-all-done = bf16[32,64,256]{2,1,0:T(8,128)(2,1)S(1)} async-done(((bf16[32,64,256]{2,1,0:T(8,128)(2,1)}), bf16[32,64,256]{2,1,0:T(8,128)(2,1)S(1)}, u32[]{:S(2)}, u32[]{:S(2)}) %all-to-all-start) | async-done | bytes 1048608 | tf_op jit(solution)/shard_map/all_to_all | solution.py:24
  49.5 0.0 copy-start.1
  49.5 50.8 %while.12 = (s32[]{:T(128)}, bf16[4,512,8192]{2,1,0:T(8,128)(2,1)}, bf16[4,512,256]{2,1,0:T(8,128)(2,1)S(1)}, f32[8192]{0:T(1024)S(1)}, bf16[8192,256]{1,0:T(8,128)(2,1)}, /*index=5*/s32[]{:T(128)}) while((s32[]{:T(128)}, bf16[4,512,8192]{2,1,0:T(8,128)(2,1)}, bf16[4,512,256]{2,1,0:T(8,128)(2,1)S(1)}, f32[8192]{0:T(1024)S(1)}, ...), condition=%wide.region_4.5_spmd, body=%wide.region_2.4_spmd.sunk | while | flops 2168847872 | bytes 13145161 | solution.py:35
  49.5 0.1 multiply_reduce_fusion.3
  49.7 12.6 %fusion.22 = bf16[4,512,8192]{2,1,0:T(8,128)(2,1)} fusion(bf16[4,512,8192]{2,1,0:T(8,128)(2,1)} %get-tuple-element.120, s32[]{:T(128)} %get-tuple-element.119, bf16[8192,256]{1,0:T(8,128)(2,1)} %get-tuple-element.129, f32[8192]{0:T(1024)S(1)} %get-tuple-element.128, f32[512]{0:T(512)S(1)} %multiply_reduce_fusion.3, ...), kind=kOutput, calls=%fused_computation.5.clone.1 | convolution fusion | flops 2168455168 | bytes 12880896 | tf_op jit(solution)/shard_map/while/body/eval_jaxpr/dot_general | solution.py:31
  62.3 0.1 multiply_reduce_fusion.3
  62.4 12.6 %fusion.22 = bf16[4,512,8192]{2,1,0:T(8,128)(2,1)} fusion(bf16[4,512,8192]{2,1,0:T(8,128)(2,1)} %get-tuple-element.120, s32[]{:T(128)} %get-tuple-element.119, bf16[8192,256]{1,0:T(8,128)(2,1)} %get-tuple-element.129, f32[8192]{0:T(1024)S(1)} %get-tuple-element.128, f32[512]{0:T(512)S(1)} %multiply_reduce_fusion.3, ...), kind=kOutput, calls=%fused_computation.5.clone.1 | convolution fusion | flops 2168455168 | bytes 12880896 | tf_op jit(solution)/shard_map/while/body/eval_jaxpr/dot_general | solution.py:31
  75.0 0.1 multiply_reduce_fusion.3
  75.1 12.6 %fusion.22 = bf16[4,512,8192]{2,1,0:T(8,128)(2,1)} fusion(bf16[4,512,8192]{2,1,0:T(8,128)(2,1)} %get-tuple-element.120, s32[]{:T(128)} %get-tuple-element.119, bf16[8192,256]{1,0:T(8,128)(2,1)} %get-tuple-element.129, f32[8192]{0:T(1024)S(1)} %get-tuple-element.128, f32[512]{0:T(512)S(1)} %multiply_reduce_fusion.3, ...), kind=kOutput, calls=%fused_computation.5.clone.1 | convolution fusion | flops 2168455168 | bytes 12880896 | tf_op jit(solution)/shard_map/while/body/eval_jaxpr/dot_general | solution.py:31
  87.7 0.1 multiply_reduce_fusion.3
  87.8 12.5 %fusion.22 = bf16[4,512,8192]{2,1,0:T(8,128)(2,1)} fusion(bf16[4,512,8192]{2,1,0:T(8,128)(2,1)} %get-tuple-element.120, s32[]{:T(128)} %get-tuple-element.119, bf16[8192,256]{1,0:T(8,128)(2,1)} %get-tuple-element.129, f32[8192]{0:T(1024)S(1)} %get-tuple-element.128, f32[512]{0:T(512)S(1)} %multiply_reduce_fusion.3, ...), kind=kOutput, calls=%fused_computation.5.clone.1 | convolution fusion | flops 2168455168 | bytes 12880896 | tf_op jit(solution)/shard_map/while/body/eval_jaxpr/dot_general | solution.py:31
  100.4 0.0 copy-done.1
  100.4 0.0 copy-start.3
  100.4 15.7 %convolution_bitcast_fusion = f32[16,2048]{1,0:T(8,128)} fusion(bf16[2048,8192]{1,0:T(8,128)(2,1)} %bitcast.28, f32[16,8192]{1,0:T(8,128)S(1)} %copy-done.1), kind=kOutput, calls=%fused_computation.11 | convolution fusion | flops 537001984 | bytes 34209792 | tf_op jit(solution)/shard_map/dot_general | solution.py:38
  116.0 0.0 all-reduce.2.cloned.1.call-update
  116.1 0.0 copy-start.4
  116.1 143.0 %all-reduce.2.cloned.1.call-done = f32[16,2048]{1,0:T(8,128)} async-done(((f32[16,2048]{1,0:T(8,128)}), f32[16,2048]{1,0:T(8,128)}) %all-reduce.2.cloned.1.call-update) | async-done | bytes 131088 | tf_op jit(solution)/shard_map/psum | solution.py:41
  259.1 0.0 copy-done.3
  259.1 0.0 copy-start.2
  259.1 14.8 %multiply_subtract_fusion = (f32[16,8192]{1,0:T(8,128)S(1)}, f32[16,8192]{1,0:T(8,128)S(1)}) fusion(f32[16,8192]{1,0:T(8,128)S(1)} %copy-done.1, bf16[2048,8192]{1,0:T(8,128)(2,1)} %bitcast.29, f32[16,2048]{1,0:T(8,128)} %all-reduce.2.cloned.1.call-done, f32[16,2048]{1,0:T(8,128)S(1)} %copy-done.3), kind=kOutput, calls=%fused_computation.14 | convolution fusion | flops 537198592 | bytes 35389440 | tf_op jit(solution)/shard_map/dot_general | solution.py:43
  274.0 2.6 copy.10
  276.6 2.8 gather_fusion.1
  279.3 0.0 copy-done
  279.3 0.2 fusion.10
  279.5 63.4 %psum.23 = f32[16,128]{1,0:T(8,128)S(1)} all-reduce(f32[16,128]{1,0:T(8,128)S(1)} %fusion.10), channel_id=1, replica_groups=mesh['loader'=4,'centers'=32] {'loader','centers'}, use_global_device_ids=true, to_apply=%region_6.7 | all-reduce | flops 2048 | bytes 16384 | tf_op jit(solution)/shard_map/psum | solution.py:48
  343.0 0.0 copy-done.4
  343.0 0.1 fusion.5
  343.1 0.1 copy.12
  343.2 2.6 copy.11
  345.8 4.9 %scatter_fusion = f32[16,8192]{0,1:T(8,128)} fusion(f32[16,8192]{0,1:T(8,128)} %copy.11, s32[64]{0:T(128)S(1)} %compare_select_fusion, f32[64,16]{1,0:T(8,128)S(1)} %copy.12), kind=kCustom, calls=%fused_computation.2 | custom fusion | flops 1024 | bytes 12544 | tf_op jit(solution)/shard_map/scatter-add | solution.py:56
  350.8 3.5 copy.13
  354.3 0.0 copy-done.2
  354.3 0.7 copy.25
  (3 shorter events, 0.0 us)
Async XLA Ops:
  7.2 272.2 %copy-start = (f32[64,128]{1,0:T(8,128)S(1)}, f32[64,128]{1,0:T(8,128)}, u32[]{:S(2)}) copy-start(f32[64,128]{1,0:T(8,128)} %param.16) | copy-start | bytes 98308
  28.3 21.2 %all-to-all-start = ((bf16[32,64,256]{2,1,0:T(8,128)(2,1)}), bf16[32,64,256]{2,1,0:T(8,128)(2,1)S(1)}, u32[]{:S(2)}, u32[]{:S(2)}) async-start(bf16[32,64,256]{2,1,0:T(8,128)(2,1)} %stack.2), calls=%async_computation | async-start | bytes 2097152 | tf_op jit(solution)/shard_map/all_to_all | solution.py:24
  36.0 223.1 %all-reduce.2.cloned.1.call-start = ((), (), s32[]{:S(2)}) async-start(), calls=%async_computation.1 | async-start | bytes 262144 | tf_op jit(solution)/shard_map/psum | solution.py:41
  49.5 50.8 %copy-start.1 = (f32[16,8192]{1,0:T(8,128)S(1)}, f32[16,8192]{1,0:T(8,128)}, u32[]{:S(2)}) copy-start(f32[16,8192]{1,0:T(8,128)} %param.14) | copy-start | bytes 1572868
  100.4 158.7 %copy-start.3 = (f32[16,2048]{1,0:T(8,128)S(1)}, f32[16,2048]{1,0:T(8,128)}, u32[]{:S(2)}) copy-start(f32[16,2048]{1,0:T(8,128)} %param.12) | copy-start | bytes 393220
  116.1 226.9 %copy-start.4 = (f32[128]{0:T(128)S(1)}, f32[128]{0:T(128)}, u32[]{:S(2)}) copy-start(f32[128]{0:T(128)} %param.17) | copy-start | bytes 1540
  259.1 95.2 %copy-start.2 = (f32[16,2048]{1,0:T(8,128)S(1)}, f32[16,2048]{1,0:T(8,128)}, u32[]{:S(2)}) copy-start(f32[16,2048]{1,0:T(8,128)} %all-reduce.2.cloned.1.call-done) | copy-start | bytes 393220
Sparse Core Ops, SparseCore 0:
  116.2 142.8 all-reduce.1
